TPU v7x, 32 devices: a whole 2x2x4 slice. The times are simulated.
32 devices in a mesh: dp: 8 (over z, x), pipe: 2 (over y), tensor: 2 (over core).
Axes of the slice: x: 2, y: 2, z: 4, core: 2. Of those that a mesh axis runs over, the one named last changes fastest.
Arguments:
- query_states: bfloat16 [2, 512, 4096], P('pipe', 'dp', 'tensor'), may hold values from -6 to 6
- passage_hidden_states: bfloat16 [2, 1440, 4096], P('pipe', 'dp', 'tensor'), may hold values from -6 to 6
- w_query: bfloat16 [2, 4096, 4096], P('pipe', 'dp', 'tensor'), may hold values from -0.09375 to 0.09375
- key_matrix: bfloat16 [2, 4096, 1024], P('pipe', 'dp', 'tensor'), may hold values from -0.09375 to 0.09375
- value_matrix: bfloat16 [2, 4096, 1024], P('pipe', 'dp', 'tensor'), may hold values from -0.09375 to 0.09375
- w_out: bfloat16 [2, 4096, 4096], P('pipe', 'tensor', 'dp'), may hold values from -0.09375 to 0.09375
- final_gain: bfloat16 [4096], P('tensor'), may hold values from 0.5 to 2
- w_vector: bfloat16 [4096, 128], P('tensor'), may hold values from -0.09375 to 0.09375
- lengths: int32 [8], P('dp'), may hold values from 1 to 180, 896 in all
- teacher: float32 [16, 8], P(('dp', 'pipe')), may hold values from -12 to 12
Outputs:
- boundary_queries: bfloat16 [2, 512, 4096], P('pipe', 'dp', 'tensor')
- boundary_passages: bfloat16 [2, 1440, 4096], P('pipe', 'dp', 'tensor')
- scores: float32 [16, 8], P(('dp', 'pipe'))
- divergence: float32 [16], P(('dp', 'pipe'))
Inputs may be any that keep to these rules, and one draw needn't show every extreme that they name: Each passage's valid tokens come first; slots after lengths[p] are padding. Some passage fills all 180 slots.
All inputs are finite; a program needn't handle non-finite values. No bound on the sum of `lengths` on one device may be relied on, other than what follows from the above.
Results may differ from a plain program's by a relative error of at most 0.0075.
Values may be sent and summed in bfloat16 or wider, within the bound.
A program may use at most 128 MiB of HBM per device.

v0:
```python
import jax
import jax.numpy as jnp
from jax import lax
from jax.sharding import PartitionSpec as P

MODEL_WIDTH = 4096
HEAD_WIDTH = 128
VEC = 128
QLEN = 32
PLEN = 180
norm_epsilon = 1e-05
vector_epsilon = 1e-06
rope_base = 10000.0


def from_root(array, axis, root):
    mine = lax.axis_index(axis) == root
    return lax.psum(jnp.where(mine, array, jnp.zeros_like(array)), axis)


def rotate(values_in, positions):
    half_size = values_in.shape[-1] // 2
    frequency = rope_base ** (-jnp.arange(half_size).astype(jnp.float32) / half_size)
    angles = positions.astype(jnp.float32)[:, None] * frequency[None, :]
    cosine = jnp.cos(angles)[:, None, :]
    sine = jnp.sin(angles)[:, None, :]
    first_half = values_in[..., :half_size]
    second_half = values_in[..., half_size:]
    return jnp.concatenate(
        [first_half * cosine - second_half * sine, second_half * cosine + first_half * sine],
        axis=-1,
    )


def attend(queries, keys, values_in):
    batch_count, length, head_count, head_size = queries.shape
    key_heads = keys.shape[2]
    grouped = queries.reshape(batch_count, length, key_heads, head_count // key_heads, head_size)
    logits = jnp.einsum(
        "bskgd,bukd->bkgsu", grouped, keys, preferred_element_type=jnp.float32
    ) * head_size ** (-0.5)
    causal = jnp.arange(length)[:, None] >= jnp.arange(length)[None, :]
    weights = jnp.where(causal, jnp.exp(logits), 0.0)
    probability = (weights / jnp.sum(weights, axis=-1, keepdims=True)).astype(jnp.bfloat16)
    combined = jnp.einsum(
        "bkgsu,bukd->bskgd", probability, values_in, preferred_element_type=jnp.float32
    )
    return combined.reshape(batch_count * length, head_count * head_size).astype(jnp.bfloat16)


def by_sequence(array_in, head_number, seq_length):
    return array_in.reshape(-1, seq_length, head_number, HEAD_WIDTH)


def late_scores(query_vectors, passage_vectors, passage_lengths):
    sims = jnp.einsum(
        "qtc,psc->qtps", query_vectors, passage_vectors, preferred_element_type=jnp.float32
    )
    valid = jnp.arange(passage_vectors.shape[1])[None, :] < passage_lengths[:, None]
    masked = jnp.where(valid[None, None], sims, -3.0)
    return jnp.sum(jnp.max(masked, axis=3), axis=1)


def body(
    query_states,
    passage_hidden_states,
    w_query,
    key_matrix,
    value_matrix,
    w_out,
    final_gain,
    w_vector,
    lengths,
    teacher,
):
    query_rows = query_states[0]
    passage_rows = passage_hidden_states[0]
    query_count = query_rows.shape[0]
    joined = jnp.concatenate([query_rows, passage_rows], axis=0)
    widened = joined.astype(jnp.float32)
    squares = jnp.sum(widened * widened, axis=1)
    total = lax.psum(squares, "tensor")
    normed_local = (widened * lax.rsqrt(total / MODEL_WIDTH + norm_epsilon)[:, None]).astype(
        jnp.bfloat16
    )
    normed = lax.all_gather(normed_local, "tensor", axis=1, tiled=True)
    query_cols = w_query.shape[2]
    key_cols = key_matrix.shape[2]
    pieces = (
        lax.all_gather(w_query[0], "dp", axis=0, tiled=True),
        lax.all_gather(key_matrix[0], "dp", axis=0, tiled=True),
        lax.all_gather(value_matrix[0], "dp", axis=0, tiled=True),
    )
    queries, keys, unprojected_values = tuple(
        (jnp.dot(normed, piece, preferred_element_type=jnp.float32) for piece in pieces)
    )
    values_out = unprojected_values.astype(jnp.bfloat16)
    query_heads = query_cols // HEAD_WIDTH
    key_heads = key_cols // HEAD_WIDTH
    query_pos = jnp.arange(QLEN)
    passage_pos = jnp.arange(PLEN)
    short_q = rotate(by_sequence(queries[:query_count], query_heads, QLEN), query_pos).astype(
        jnp.bfloat16
    )
    short_k = rotate(by_sequence(keys[:query_count], key_heads, QLEN), query_pos).astype(
        jnp.bfloat16
    )
    short_v = by_sequence(values_out[:query_count], key_heads, QLEN)
    long_q = rotate(by_sequence(queries[query_count:], query_heads, PLEN), passage_pos).astype(
        jnp.bfloat16
    )
    long_k = rotate(by_sequence(keys[query_count:], key_heads, PLEN), passage_pos).astype(
        jnp.bfloat16
    )
    long_v = by_sequence(values_out[query_count:], key_heads, PLEN)
    attended = jnp.concatenate(
        [attend(short_q, short_k, short_v), attend(long_q, long_k, long_v)], axis=0
    )
    branch_full = jnp.dot(
        attended,
        lax.all_gather(w_out[0], "dp", axis=1, tiled=True),
        preferred_element_type=jnp.float32,
    )
    branch = lax.psum_scatter(
        branch_full.astype(jnp.bfloat16), "tensor", scatter_dimension=1, tiled=True
    ).astype(jnp.float32)
    updated = (widened + branch).astype(jnp.bfloat16)
    boundary_queries = updated[:query_count][None]
    boundary_passages = updated[query_count:][None]
    scaled = (updated.astype(jnp.float32) * final_gain.astype(jnp.float32)[None, :]).astype(
        jnp.bfloat16
    )
    partial_vec = jnp.dot(scaled, w_vector, preferred_element_type=jnp.float32)
    projected = lax.psum(partial_vec.astype(jnp.bfloat16), "tensor").astype(jnp.float32)
    vectors = (
        projected
        * lax.rsqrt(jnp.sum(projected * projected, axis=1, keepdims=True) + vector_epsilon)
    ).astype(jnp.bfloat16)
    query_vectors = vectors[:query_count].reshape(-1, QLEN, VEC)
    passage_vectors = vectors[query_count:].reshape(-1, PLEN, VEC)
    last_section = lax.axis_size("pipe") - 1
    query_vectors, passage_vectors = (
        from_root(query_vectors, "pipe", last_section),
        from_root(passage_vectors, "pipe", last_section),
    )
    owned = query_vectors.shape[0] // lax.axis_size("pipe")
    own_queries = lax.dynamic_slice_in_dim(query_vectors, lax.axis_index("pipe") * owned, owned, 0)
    pieces = (
        lax.all_gather(passage_vectors, "dp", axis=0, tiled=True),
        lax.all_gather(lengths, "dp", axis=0, tiled=True),
    )
    block = late_scores(own_queries, pieces[0], pieces[1])
    log_student = block - jnp.log(jnp.sum(jnp.exp(block), axis=1, keepdims=True))
    log_teacher = teacher - jnp.log(jnp.sum(jnp.exp(teacher), axis=1, keepdims=True))
    divergence = jnp.sum(jnp.exp(log_teacher) * (log_teacher - log_student), axis=1)
    return (boundary_queries, boundary_passages, block, divergence)


def solution(mesh):
    in_specs = (
        P("pipe", "dp", "tensor"),
        P("pipe", "dp", "tensor"),
        P("pipe", "dp", "tensor"),
        P("pipe", "dp", "tensor"),
        P("pipe", "dp", "tensor"),
        P("pipe", "tensor", "dp"),
        P("tensor"),
        P("tensor", None),
        P("dp"),
        P(("dp", "pipe"), None),
    )
    out_specs = (
        P("pipe", "dp", "tensor"),
        P("pipe", "dp", "tensor"),
        P(("dp", "pipe"), None),
        P(("dp", "pipe")),
    )
    return jax.shard_map(body, mesh=mesh, in_specs=in_specs, out_specs=out_specs, check_vma=False)
```

profile of v0, /device:TPU:0, one launch (start us, length us, event | category | flops | bytes accessed | tf_op | source)
XLA Modules:
  0.0 714.7 jit_solution(4791329132297808971)
XLA Ops:
  7.2 0.0 all-gather.10.cloned.1.call-start
  7.2 1.5 fusion.12
  8.7 2.6 psum.28
  11.3 2.4 fusion.13
  13.7 0.0 all-gather.14.cloned.1.call-start
  13.8 0.7 all-gather.14.cloned.1.call-update
  14.5 0.0 all-gather.12.cloned.1.call-start
  14.5 0.7 all-gather.12.cloned.1.call-update
  15.2 0.0 all-gather.16.cloned.1.call-start
  15.3 0.5 all-gather.16.cloned.1.call-update
  15.8 0.5 all-gather.18.cloned.1.call-update
  16.4 0.0 reduce-scatter.2.cloned.1.call-start
  16.5 0.1 multiply_cosine_fusion.1
  16.6 0.4 multiply_cosine_fusion
  17.1 9.9 %all-gather.10.cloned.1.call-done = bf16[244,4096]{1,0:T(8,128)(2,1)} async-done(((bf16[244,2048]{1,0:T(8,128)(2,1)}), bf16[244,4096]{1,0:T(8,128)(2,1)}) %all-gather.10.cloned.1.call-update) | async-done | bytes 1998864 | tf_op jit(solution)/shard_map/all_gather | solution.py:86
  26.9 76.7 %all-gather.14.cloned.1.call-done = bf16[1,4096,512]{2,1,0:T(8,128)(2,1)} async-done(((bf16[1,512,512]{2,1,0:T(8,128)(2,1)}), bf16[1,4096,512]{2,1,0:T(8,128)(2,1)}) %all-gather.14.cloned.1.call-update) | async-done | bytes 4194320 | tf_op jit(solution)/shard_map/all_gather | solution.py:91
  103.7 4.0 fusion.7
  107.7 69.8 %all-gather.12.cloned.1.call-done = bf16[1,4096,512]{2,1,0:T(8,128)(2,1)} async-done(((bf16[1,512,512]{2,1,0:T(8,128)(2,1)}), bf16[1,4096,512]{2,1,0:T(8,128)(2,1)}) %all-gather.12.cloned.1.call-update) | async-done | bytes 4194320 | tf_op jit(solution)/shard_map/all_gather | solution.py:92
  177.5 4.0 fusion.27
  181.5 0.1 reshape.284
  181.7 0.7 reshape.283
  182.5 0.1 fusion.65
  182.7 0.3 fusion.64
  182.9 0.1 fusion.44
  183.0 222.4 %all-gather.16.cloned.1.call-done = bf16[1,4096,2048]{2,1,0:T(8,128)(2,1)} async-done(((bf16[1,512,2048]{2,1,0:T(8,128)(2,1)}), bf16[1,4096,2048]{2,1,0:T(8,128)(2,1)}) %all-gather.16.cloned.1.call-update) | async-done | bytes 16777232 | tf_op jit(solution)/shard_map/all_gather | solution.py:90
  405.4 8.6 %fusion.2 = f32[244,2048]{1,0:T(8,128)S(1)} fusion(bf16[244,4096]{1,0:T(8,128)(2,1)} %all-gather.10.cloned.1.call-done, bf16[1,4096,2048]{2,1,0:T(8,128)(2,1)} %all-gather.16.cloned.1.call-done), kind=kOutput, calls=%fused_computation.2 | convolution fusion | flops 4093640704 | bytes 20774912 | tf_op jit(solution)/shard_map/dot_general | solution.py:95
  414.0 0.1 slice.83
  414.2 0.3 copy.69
  414.4 0.1 slice_bitcast_fusion
  414.5 0.7 subtract_convert_fusion
  415.2 0.2 copy.49
  415.4 0.2 copy.50
  415.7 1.3 fusion.11
  417.0 1.0 fusion.21
  418.0 0.3 copy.53
  418.3 1.3 convert_element_type.173
  419.6 0.1 copy.68
  419.7 0.2 subtract_convert_fusion.1
  420.0 0.1 copy.42
  420.0 0.1 copy.43
  420.1 0.6 fusion.26
  420.7 0.3 fusion.30
  421.0 0.1 copy.46
  421.2 0.2 convert_element_type.167
  421.4 211.9 %all-gather.18.cloned.1.call-done = bf16[1,2048,4096]{2,1,0:T(8,128)(2,1)} async-done(((bf16[1,2048,512]{2,1,0:T(8,128)(2,1)}), bf16[1,2048,4096]{2,1,0:T(8,128)(2,1)}) %all-gather.18.cloned.1.call-update) | async-done | bytes 16777232 | tf_op jit(solution)/shard_map/all_gather | solution.py:121
  633.2 11.6 %fusion.4 = bf16[244,4096]{1,0:T(8,128)(2,1)} fusion(bf16[1,2048,4096]{2,1,0:T(8,128)(2,1)} %all-gather.18.cloned.1.call-done, bf16[180,2048]{1,0:T(8,128)(2,1)S(1)} %copy-done.3, bf16[64,2048]{1,0:T(8,128)(2,1)S(1)} %convert_element_type.167), kind=kOutput, calls=%fused_computation.4 | convolution fusion | flops 4096638976 | bytes 19775488 | tf_op jit(solution)/shard_map/dot_general | solution.py:119
  645.7 0.6 dynamic-slice
  646.2 0.8 dynamic-update-slice
  647.0 9.5 %all-reduce = s32[8]{0:T(128)S(1)} all-reduce(s32[8]{0:T(128)S(1)} %dynamic-update-slice), channel_id=1, replica_groups=mesh['dp'=8,'pipe'=2,'tensor'=2] {'dp'}, use_global_device_ids=true, to_apply=%add | all-reduce | flops 8 | bytes 64
  656.5 0.6 exponential_reduce_fusion.1
  657.8 0.1 iota_compare_fusion.2
  657.9 1.6 fusion.14
  659.5 0.4 convolution_convert_fusion.1
  659.9 3.6 psum.29
  663.5 0.1 fusion.49
  663.6 0.1 fusion.50
  663.8 0.9 slice_bitcast_fusion.1
  664.7 0.7 slice_bitcast_fusion.3
  665.4 8.8 %all-reduce.1 = (bf16[1,180,128]{2,1,0:T(8,128)(2,1)S(1)}, bf16[2,32,128]{2,1,0:T(8,128)(2,1)S(1)}) all-reduce(bf16[1,180,128]{2,1,0:T(8,128)(2,1)S(1)} %fusion.54, bf16[2,32,128]{2,1,0:T(8,128)(2,1)S(1)} %bitcast.117), channel_id=1, replica_groups=mesh['dp'=8,'pipe'=2,'tensor'=2] {'pipe'}, use_global_device_ids=true, to_apply=%region_8.9 | all-reduce | flops 31232 | bytes 124928 | tf_op jit(solution)/shard_map/psum | solution.py:18
  674.2 31.2 %all_gather.27 = bf16[8,180,128]{2,1,0:T(8,128)(2,1)S(1)} all-gather(bf16[1,180,128]{2,1,0:T(8,128)(2,1)S(1)} %get-tuple-element.4), channel_id=1, replica_groups=mesh['dp'=8,'pipe'=2,'tensor'=2] {'dp'}, dimensions={0}, use_global_device_ids=true | all-gather | bytes 414720 | tf_op jit(solution)/shard_map/all_gather | solution.py:149
  705.4 0.4 fusion.31
  705.8 0.1 reduce_sum.80
  705.9 0.6 exponential_reduce_fusion
  707.2 0.6 multiply_reduce_fusion
  (41 shorter events, 0.4 us)
Async XLA Ops:
  7.2 652.3 %copy-start = (bf16[2048,128]{1,0:T(8,128)(2,1)S(1)}, bf16[2048,128]{1,0:T(8,128)(2,1)}, u32[]{:S(2)}) copy-start(bf16[2048,128]{1,0:T(8,128)(2,1)} %param.17) | copy-start | bytes 1572868
  7.2 19.8 %all-gather.10.cloned.1.call-start = ((), (), s32[]{:S(2)}) async-start(), calls=%async_computation.1 | async-start | bytes 3047424 | tf_op jit(solution)/shard_map/all_gather | solution.py:86
  13.7 89.9 %all-gather.14.cloned.1.call-start = ((), (), s32[]{:S(2)}) async-start(), calls=%async_computation.4 | async-start | bytes 4718592 | tf_op jit(solution)/shard_map/all_gather | solution.py:91
  14.5 163.0 %all-gather.12.cloned.1.call-start = ((), (), s32[]{:S(2)}) async-start(), calls=%async_computation.3 | async-start | bytes 4718592 | tf_op jit(solution)/shard_map/all_gather | solution.py:92
  15.2 390.2 %all-gather.16.cloned.1.call-start = ((), (), s32[]{:S(2)}) async-start(), calls=%async_computation.5 | async-start | bytes 18874368 | tf_op jit(solution)/shard_map/all_gather | solution.py:90
  15.8 617.5 %all-gather.18.cloned.1.call-start = ((), (), s32[]{:S(2)}) async-start(), calls=%async_computation.6 | async-start | bytes 18874368 | tf_op jit(solution)/shard_map/all_gather | solution.py:121
  16.4 641.5 %reduce-scatter.2.cloned.1.call-start = ((), (), s32[]{:S(2)}) async-start(), calls=%async_computation.2 | async-start | bytes 3047424 | tf_op jit(solution)/shard_map/reduce_scatter | solution.py:124
  415.6 1.3 copy-start.4
  420.1 213.1 %copy-start.3 = (bf16[180,2048]{1,0:T(8,128)(2,1)S(1)}, bf16[180,2048]{1,0:T(8,128)(2,1)}, u32[]{:S(2)}) copy-start(bf16[180,2048]{1,0:T(8,128)(2,1)} %convert_element_type.173) | copy-start | bytes 2211844
  644.9 0.8 copy-start.8
  644.9 11.6 %copy-start.5 = (bf16[2048]{0:T(1024)(128)(2,1)S(1)}, bf16[2048]{0:T(1024)(128)(2,1)}, u32[]{:S(2)}) copy-start(bf16[2048]{0:T(1024)(128)(2,1)} %param.16) | copy-start | bytes 12292
  644.9 11.6 %copy-start.7 = (f32[1,8]{1,0:T(1,128)S(1)}, f32[1,8]{1,0:T(1,128)}, u32[]{:S(2)}) copy-start(f32[1,8]{1,0:T(1,128)} %param.19) | copy-start | bytes 100
  644.9 13.0 %copy-start.1 = (bf16[1,180,2048]{2,1,0:T(8,128)(2,1)S(1)}, bf16[1,180,2048]{2,1,0:T(8,128)(2,1)}, u32[]{:S(2)}) copy-start(bf16[1,180,2048]{2,1,0:T(8,128)(2,1)} %param.11) | copy-start | bytes 2211844
  644.9 13.0 %copy-start.2 = (bf16[1,64,2048]{2,1,0:T(8,128)(2,1)S(1)}, bf16[1,64,2048]{2,1,0:T(8,128)(2,1)}, u32[]{:S(2)}) copy-start(bf16[1,64,2048]{2,1,0:T(8,128)(2,1)} %param.10) | copy-start | bytes 786436
  705.9 1.9 copy-start.6
Sparse Core Ops, SparseCore 0:
  13.8 13.0 all-gather.9
  29.1 74.5 all-gather.13
  105.8 71.6 all-gather.11
  179.5 225.8 all-gather.15
  407.3 225.9 all-gather.17
  645.0 7.7 reduce-scatter.1
where the time goes:
time: 715 us
  waiting for transfers between devices  593 us (83%)
  blocking collectives  55.6 us (8%)
  matrix products  32.3 us (5%)
  between operations  16.6 us (2%)
  other arithmetic  9.36 us (1%)
  local copies, waits for them, and re-layouts  7.48 us (1%)
    all_gather x1, waiting for transfers between devices, body(): lax.all_gather(w_query[0], 'dp', axis=0, tiled=True)  222 us
    all_gather x1, waiting for transfers between devices, body(): lax.all_gather(w_out[0], 'dp', axis=1, tiled=True)  212 us
    all_gather x1, waiting for transfers between devices, body(): lax.all_gather(key_matrix[0], 'dp', axis=0, tiled=True)  76.7 us
    all_gather x1, waiting for transfers between devices, body(): lax.all_gather(value_matrix[0], 'dp', axis=0, tiled=True)  69.8 us
    all_gather x1, blocking collectives, body(): lax.all_gather(passage_vectors, 'dp', axis=0, tiled=True)  31.2 us
    dot_general x3, matrix products, body(): jnp.dot(normed, piece, preferred_element_type=jnp.float32)  16.7 us
  transfers between devices with their start and end apart: 6, of which 5 were waited for; matrix products, arithmetic and copies ran while one was open for 4% of the time, Pallas kernels for 0%

commit v1 on v0

--- a/solution.py
+++ b/solution.py
@@ -11,6 +11,19 @@
 norm_epsilon = 1e-05
 vector_epsilon = 1e-06
 rope_base = 10000.0
+
+
+def gather_around(array, axis, dim):
+    devices, mine, rows = (lax.axis_size(axis), lax.axis_index(axis), array.shape[dim])
+    right = [(i, (i + 1) % devices) for i in range(devices)]
+    out = jnp.zeros((*array.shape[:dim], devices * rows, *array.shape[dim + 1 :]), array.dtype)
+    carried = array
+    for step in range(devices):
+        holder = (mine - step) % devices
+        out = lax.dynamic_update_slice_in_dim(out, carried, holder * rows, axis=dim)
+        if step < devices - 1:
+            carried = lax.ppermute(carried, axis, right)
+    return out
 
 
 def from_root(array, axis, root):
@@ -89,7 +102,7 @@
     pieces = (
         lax.all_gather(w_query[0], "dp", axis=0, tiled=True),
         lax.all_gather(key_matrix[0], "dp", axis=0, tiled=True),
-        lax.all_gather(value_matrix[0], "dp", axis=0, tiled=True),
+        gather_around(value_matrix[0], "dp", 0),
     )
     queries, keys, unprojected_values = tuple(
         (jnp.dot(normed, piece, preferred_element_type=jnp.float32) for piece in pieces)

time: 715 us -> 686 us (0.959)
  waiting for transfers between devices: 593 us -> 548 us
  local copies, waits for them, and re-layouts: 7.48 us -> 19.8 us
    ppermute x0 -> x7, waiting for transfers between devices: none -> 145 us  [gather_around(): carried = lax.ppermute(carried, axis, right)]
    all_gather x1, waiting for transfers between devices: 76.7 us -> 0.01 us  [body(): lax.all_gather(key_matrix[0], 'dp', axis=0, tiled=True)]
    all_gather x1 -> x0, waiting for transfers between devices: 69.8 us -> none  [body(): lax.all_gather(value_matrix[0], 'dp', axis=0, tiled=True)]
    all_gather x1, waiting for transfers between devices: 222 us -> 190 us  [body(): lax.all_gather(w_query[0], 'dp', axis=0, tiled=True)]
    all_gather x1, waiting for transfers between devices: 9.89 us -> 0.01 us  [body(): normed = lax.all_gather(normed_local, 'tensor', axis=1, tiled=True)]
    dynamic_update_slice x0 -> x8, local copies, waits for them, and re-layouts: none -> 8.86 us  [gather_around(): out = lax.dynamic_update_slice_in_dim(out, carried, holder * rows, axis=dim)]
  transfers between devices with their start and end apart: 6 -> 12, of which waited for: 5 -> 9; matrix products, arithmetic and copies ran while one was open for 4% -> 6% of each run, Pallas kernels for 0% -> 0%
where the time goes in v1:
time: 686 us; the launch traced here: 685 us
  waiting for transfers between devices  548 us (80%)
  blocking collectives  55.6 us (8%)
  matrix products  32.4 us (5%)
  local copies, waits for them, and re-layouts  19.8 us (3%)
  between operations  16.5 us (2%)
  other arithmetic  9.39 us (1%)
    all_gather x1, waiting for transfers between devices, body(): lax.all_gather(w_out[0], 'dp', axis=1, tiled=True)  211 us
    all_gather x1, waiting for transfers between devices, body(): lax.all_gather(w_query[0], 'dp', axis=0, tiled=True)  190 us
    ppermute x7, waiting for transfers between devices, gather_around(): carried = lax.ppermute(carried, axis, right)  145 us
    all_gather x1, blocking collectives, body(): lax.all_gather(passage_vectors, 'dp', axis=0, tiled=True)  31.2 us
    dot_general x3, matrix products, body(): jnp.dot(normed, piece, preferred_element_type=jnp.float32)  16.8 us
  transfers between devices with their start and end apart: 12, of which 9 were waited for; matrix products, arithmetic and copies ran while one was open for 6% of the time, Pallas kernels for 0%

profile of v1, /device:TPU:0, one launch (start us, length us, event | category | flops | bytes accessed | tf_op | source)
XLA Modules:
  0.0 685.2 jit_solution(6613265457260279007)
XLA Ops:
  7.2 1.5 fusion.10
  8.7 2.6 psum.28
  11.3 2.4 fusion.11
  13.8 0.7 all-gather.10.cloned.1.call-update
  14.6 0.7 all-gather.12.cloned.1.call-update
  15.3 0.5 all-gather.14.cloned.1.call-update
  15.9 2.9 collective-permute-start
  18.8 15.3 %collective-permute-done = bf16[512,512]{1,0:T(8,128)(2,1)S(1)} collective-permute-done((bf16[512,512]{1,0:T(8,128)(2,1)S(1)}, bf16[512,512]{1,0:T(8,128)(2,1)S(1)}, u32[]{:S(2)}, u32[]{:S(2)}) %collective-permute-start) | collective-permute-done | bytes 524320 | tf_op jit(solution)/shard_map/ppermute | solution.py:25
  34.1 23.6 %collective-permute-done.1 = bf16[512,512]{1,0:T(8,128)(2,1)S(1)} collective-permute-done((bf16[512,512]{1,0:T(8,128)(2,1)S(1)}, bf16[512,512]{1,0:T(8,128)(2,1)S(1)}, u32[]{:S(2)}, u32[]{:S(2)}) %collective-permute-start.1) | collective-permute-done | bytes 524320 | tf_op jit(solution)/shard_map/ppermute | solution.py:25
  57.7 20.7 %collective-permute-done.2 = bf16[512,512]{1,0:T(8,128)(2,1)S(1)} collective-permute-done((bf16[512,512]{1,0:T(8,128)(2,1)S(1)}, bf16[512,512]{1,0:T(8,128)(2,1)S(1)}, u32[]{:S(2)}, u32[]{:S(2)}) %collective-permute-start.2) | collective-permute-done | bytes 524320 | tf_op jit(solution)/shard_map/ppermute | solution.py:25
  78.4 27.9 %collective-permute-done.3 = bf16[512,512]{1,0:T(8,128)(2,1)S(1)} collective-permute-done((bf16[512,512]{1,0:T(8,128)(2,1)S(1)}, bf16[512,512]{1,0:T(8,128)(2,1)S(1)}, u32[]{:S(2)}, u32[]{:S(2)}) %collective-permute-start.3) | collective-permute-done | bytes 524320 | tf_op jit(solution)/shard_map/ppermute | solution.py:25
  106.3 0.8 copy-done.5
  107.1 0.1 multiply_cosine_fusion.1
  107.2 0.4 multiply_cosine_fusion
  107.6 26.3 %collective-permute-done.4 = bf16[512,512]{1,0:T(8,128)(2,1)} collective-permute-done((bf16[512,512]{1,0:T(8,128)(2,1)S(1)}, bf16[512,512]{1,0:T(8,128)(2,1)}, u32[]{:S(2)}, u32[]{:S(2)}) %collective-permute-start.4) | collective-permute-done | bytes 524320 | tf_op jit(solution)/shard_map/ppermute | solution.py:25
  134.1 2.2 broadcast_in_dim.34
  136.4 0.8 constant_dynamic-update-slice_fusion.7
  137.2 0.8 constant_dynamic-update-slice_fusion.6
  138.0 11.4 %collective-permute-done.5 = bf16[512,512]{1,0:T(8,128)(2,1)} collective-permute-done((bf16[512,512]{1,0:T(8,128)(2,1)}, bf16[512,512]{1,0:T(8,128)(2,1)}, u32[]{:S(2)}, u32[]{:S(2)}) %collective-permute-start.5) | collective-permute-done | bytes 524320 | tf_op jit(solution)/shard_map/ppermute | solution.py:25
  149.4 0.8 constant_dynamic-update-slice_fusion.5
  150.3 0.8 constant_dynamic-update-slice_fusion.4
  151.1 0.9 constant_dynamic-update-slice_fusion.3
  152.0 2.0 constant_dynamic-update-slice_fusion.2
  153.9 1.9 constant_dynamic-update-slice_fusion.1
  155.8 19.5 %collective-permute-done.6 = bf16[512,512]{1,0:T(8,128)(2,1)S(1)} collective-permute-done((bf16[512,512]{1,0:T(8,128)(2,1)}, bf16[512,512]{1,0:T(8,128)(2,1)S(1)}, u32[]{:S(2)}, u32[]{:S(2)}) %collective-permute-start.6) | collective-permute-done | bytes 524320 | tf_op jit(solution)/shard_map/ppermute | solution.py:25
  175.3 0.8 constant_dynamic-update-slice_fusion
  176.1 4.0 convolution_convert_fusion.1
  180.3 0.7 reshape.283
  181.0 4.1 fusion.7
  185.2 0.1 reshape.284
  185.5 0.3 fusion.59
  185.9 190.3 %all-gather.12.cloned.1.call-done = bf16[1,4096,2048]{2,1,0:T(8,128)(2,1)} async-done(((bf16[1,512,2048]{2,1,0:T(8,128)(2,1)}), bf16[1,4096,2048]{2,1,0:T(8,128)(2,1)}) %all-gather.12.cloned.1.call-update) | async-done | bytes 16777232 | tf_op jit(solution)/shard_map/all_gather | solution.py:103
  376.2 8.6 %fusion.2 = f32[244,2048]{1,0:T(8,128)S(1)} fusion(bf16[244,4096]{1,0:T(8,128)(2,1)} %all-gather.8.cloned.1.call-done, bf16[1,4096,2048]{2,1,0:T(8,128)(2,1)} %all-gather.12.cloned.1.call-done), kind=kOutput, calls=%fused_computation.2 | convolution fusion | flops 4093640704 | bytes 20774912 | tf_op jit(solution)/shard_map/dot_general | solution.py:108
  384.9 1.3 copy-done.2
  386.3 0.2 subtract_convert_fusion.1
  386.7 0.6 fusion.24
  387.3 0.3 fusion.25
  387.6 0.1 copy.46
  387.7 0.2 convert_element_type.167
  387.9 0.2 slice-done
  388.1 0.3 copy.69
  388.5 0.7 subtract_convert_fusion
  389.2 0.2 copy.49
  389.4 0.2 copy.50
  389.6 1.3 fusion.9
  390.9 1.0 fusion.19
  391.9 0.3 copy.53
  392.2 0.4 convert_element_type.173
  392.7 211.4 %all-gather.14.cloned.1.call-done = bf16[1,2048,4096]{2,1,0:T(8,128)(2,1)} async-done(((bf16[1,2048,512]{2,1,0:T(8,128)(2,1)}), bf16[1,2048,4096]{2,1,0:T(8,128)(2,1)}) %all-gather.14.cloned.1.call-update) | async-done | bytes 16777232 | tf_op jit(solution)/shard_map/all_gather | solution.py:134
  604.1 11.6 %fusion.4 = bf16[244,4096]{1,0:T(8,128)(2,1)} fusion(bf16[1,2048,4096]{2,1,0:T(8,128)(2,1)} %all-gather.14.cloned.1.call-done, bf16[180,2048]{1,0:T(8,128)(2,1)S(1)} %convert_element_type.173, bf16[64,2048]{1,0:T(8,128)(2,1)S(1)} %convert_element_type.167), kind=kOutput, calls=%fused_computation.4 | convolution fusion | flops 4096638976 | bytes 19775488 | tf_op jit(solution)/shard_map/dot_general | solution.py:132
  616.5 0.6 dynamic-slice
  617.1 0.8 dynamic-update-slice
  617.9 9.4 %all-reduce = s32[8]{0:T(128)S(1)} all-reduce(s32[8]{0:T(128)S(1)} %dynamic-update-slice), channel_id=1, replica_groups=mesh['dp'=8,'pipe'=2,'tensor'=2] {'dp'}, use_global_device_ids=true, to_apply=%add | all-reduce | flops 8 | bytes 64
  627.3 0.6 exponential_reduce_fusion.1
  628.7 1.6 fusion.12
  630.3 0.4 convolution_convert_fusion.2
  630.7 3.6 psum.29
  634.6 0.9 slice_bitcast_fusion.1
  635.5 0.7 slice_bitcast_fusion.3
  636.3 8.8 %all-reduce.1 = (bf16[1,180,128]{2,1,0:T(8,128)(2,1)S(1)}, bf16[2,32,128]{2,1,0:T(8,128)(2,1)S(1)}) all-reduce(bf16[1,180,128]{2,1,0:T(8,128)(2,1)S(1)} %fusion.49, bf16[2,32,128]{2,1,0:T(8,128)(2,1)S(1)} %bitcast.116), channel_id=1, replica_groups=mesh['dp'=8,'pipe'=2,'tensor'=2] {'pipe'}, use_global_device_ids=true, to_apply=%region_8.9 | all-reduce | flops 31232 | bytes 124928 | tf_op jit(solution)/shard_map/psum | solution.py:31
  645.1 31.2 %all_gather.23 = bf16[8,180,128]{2,1,0:T(8,128)(2,1)S(1)} all-gather(bf16[1,180,128]{2,1,0:T(8,128)(2,1)S(1)} %get-tuple-element.4), channel_id=1, replica_groups=mesh['dp'=8,'pipe'=2,'tensor'=2] {'dp'}, dimensions={0}, use_global_device_ids=true | all-gather | bytes 414720 | tf_op jit(solution)/shard_map/all_gather | solution.py:162
  676.2 0.4 fusion.26
  676.8 0.6 exponential_reduce_fusion
  678.1 0.6 multiply_reduce_fusion
  (68 shorter events, 1.6 us)
Async XLA Ops:
  7.2 623.1 %copy-start = (bf16[2048,128]{1,0:T(8,128)(2,1)S(1)}, bf16[2048,128]{1,0:T(8,128)(2,1)}, u32[]{:S(2)}) copy-start(bf16[2048,128]{1,0:T(8,128)(2,1)} %param.17) | copy-start | bytes 1572868
  7.2 169.0 %all-gather.8.cloned.1.call-start = ((), (), s32[]{:S(2)}) async-start(), calls=%async_computation.1 | async-start | bytes 3047424 | tf_op jit(solution)/shard_map/all_gather | solution.py:99
  13.8 167.2 %all-gather.10.cloned.1.call-start = ((), (), s32[]{:S(2)}) async-start(), calls=%async_computation.3 | async-start | bytes 4718592 | tf_op jit(solution)/shard_map/all_gather | solution.py:104
  14.5 1.4 copy-start.4
  14.5 361.7 %all-gather.12.cloned.1.call-start = ((), (), s32[]{:S(2)}) async-start(), calls=%async_computation.4 | async-start | bytes 18874368 | tf_op jit(solution)/shard_map/all_gather | solution.py:103
  15.2 588.8 %all-gather.14.cloned.1.call-start = ((), (), s32[]{:S(2)}) async-start(), calls=%async_computation.5 | async-start | bytes 18874368 | tf_op jit(solution)/shard_map/all_gather | solution.py:134
  15.8 612.9 %reduce-scatter.2.cloned.1.call-start = ((), (), s32[]{:S(2)}) async-start(), calls=%async_computation.2 | async-start | bytes 3047424 | tf_op jit(solution)/shard_map/reduce_scatter | solution.py:137
  15.9 18.2 %collective-permute-start = (bf16[512,512]{1,0:T(8,128)(2,1)S(1)}, bf16[512,512]{1,0:T(8,128)(2,1)S(1)}, u32[]{:S(2)}, u32[]{:S(2)}) collective-permute-start(bf16[512,512]{1,0:T(8,128)(2,1)S(1)} %bitcast.113), channel_id=1, source_target_pairs={{0,4},{4,8},{8,12},{12,16},{16,20},{20,24},{24,28},{28,0},{1,5},{5... | collective-permute-start | bytes 1572872 | tf_op jit(solution)/shard_map/ppermute | solution.py:25
  34.0 23.6 %collective-permute-start.1 = (bf16[512,512]{1,0:T(8,128)(2,1)S(1)}, bf16[512,512]{1,0:T(8,128)(2,1)S(1)}, u32[]{:S(2)}, u32[]{:S(2)}) collective-permute-start(bf16[512,512]{1,0:T(8,128)(2,1)S(1)} %collective-permute-done), channel_id=1, source_target_pairs={{0,4},{4,8},{8,12},{12,16},{16,20},{20,24},{24,28},{28,0},{1,5},{5... | collective-permute-start | bytes 1572872 | tf_op jit(solution)/shard_map/ppermute | solution.py:25
  57.7 20.7 %collective-permute-start.2 = (bf16[512,512]{1,0:T(8,128)(2,1)S(1)}, bf16[512,512]{1,0:T(8,128)(2,1)S(1)}, u32[]{:S(2)}, u32[]{:S(2)}) collective-permute-start(bf16[512,512]{1,0:T(8,128)(2,1)S(1)} %collective-permute-done.1), channel_id=1, source_target_pairs={{0,4},{4,8},{8,12},{12,16},{16,20},{20,24},{24,28},{28,0},{1,5},{5... | collective-permute-start | bytes 1572872 | tf_op jit(solution)/shard_map/ppermute | solution.py:25
  78.4 27.9 %collective-permute-start.3 = (bf16[512,512]{1,0:T(8,128)(2,1)S(1)}, bf16[512,512]{1,0:T(8,128)(2,1)S(1)}, u32[]{:S(2)}, u32[]{:S(2)}) collective-permute-start(bf16[512,512]{1,0:T(8,128)(2,1)S(1)} %collective-permute-done.2), channel_id=1, source_target_pairs={{0,4},{4,8},{8,12},{12,16},{16,20},{20,24},{24,28},{28,0},{1,5},{5... | collective-permute-start | bytes 1572872 | tf_op jit(solution)/shard_map/ppermute | solution.py:25
  106.3 0.8 copy-start.5
  106.3 27.6 %collective-permute-start.4 = (bf16[512,512]{1,0:T(8,128)(2,1)S(1)}, bf16[512,512]{1,0:T(8,128)(2,1)}, u32[]{:S(2)}, u32[]{:S(2)}) collective-permute-start(bf16[512,512]{1,0:T(8,128)(2,1)S(1)} %collective-permute-done.3), channel_id=1, source_target_pairs={{0,4},{4,8},{8,12},{12,16},{16,20},{20,24},{24,28},{28,0},{1,5},{5... | collective-permute-start | bytes 1572872 | tf_op jit(solution)/shard_map/ppermute | solution.py:25
  133.9 15.5 %collective-permute-start.5 = (bf16[512,512]{1,0:T(8,128)(2,1)}, bf16[512,512]{1,0:T(8,128)(2,1)}, u32[]{:S(2)}, u32[]{:S(2)}) collective-permute-start(bf16[512,512]{1,0:T(8,128)(2,1)} %collective-permute-done.4), channel_id=1, source_target_pairs={{0,4},{4,8},{8,12},{12,16},{16,20},{20,24},{24,28},{28,0},{1,5},{5... | collective-permute-start | bytes 1572872 | tf_op jit(solution)/shard_map/ppermute | solution.py:25
  136.4 14.7 %copy-start.6 = (bf16[512,512]{1,0:T(8,128)(2,1)S(1)}, bf16[512,512]{1,0:T(8,128)(2,1)}, u32[]{:S(2)}) copy-start(bf16[512,512]{1,0:T(8,128)(2,1)} %copy-done.5) | copy-start | bytes 1572868
  149.4 25.9 %collective-permute-start.6 = (bf16[512,512]{1,0:T(8,128)(2,1)}, bf16[512,512]{1,0:T(8,128)(2,1)S(1)}, u32[]{:S(2)}, u32[]{:S(2)}) collective-permute-start(bf16[512,512]{1,0:T(8,128)(2,1)} %collective-permute-done.5), channel_id=1, source_target_pairs={{0,4},{4,8},{8,12},{12,16},{16,20},{20,24},{24,28},{28,0},{1,5},{5... | collective-permute-start | bytes 1572872 | tf_op jit(solution)/shard_map/ppermute | solution.py:25
  384.9 1.3 copy-start.2
  386.7 1.4 slice-start
  389.6 1.3 copy-start.7
  615.7 0.8 copy-start.11
  615.7 11.6 %copy-start.8 = (bf16[2048]{0:T(1024)(128)(2,1)S(1)}, bf16[2048]{0:T(1024)(128)(2,1)}, u32[]{:S(2)}) copy-start(bf16[2048]{0:T(1024)(128)(2,1)} %param.16) | copy-start | bytes 12292
  615.7 11.6 %copy-start.10 = (f32[1,8]{1,0:T(1,128)S(1)}, f32[1,8]{1,0:T(1,128)}, u32[]{:S(2)}) copy-start(f32[1,8]{1,0:T(1,128)} %param.19) | copy-start | bytes 100
  615.7 13.0 %copy-start.1 = (bf16[1,180,2048]{2,1,0:T(8,128)(2,1)S(1)}, bf16[1,180,2048]{2,1,0:T(8,128)(2,1)}, u32[]{:S(2)}) copy-start(bf16[1,180,2048]{2,1,0:T(8,128)(2,1)} %param.11) | copy-start | bytes 2211844
  615.7 13.0 %copy-start.3 = (bf16[1,64,2048]{2,1,0:T(8,128)(2,1)S(1)}, bf16[1,64,2048]{2,1,0:T(8,128)(2,1)}, u32[]{:S(2)}) copy-start(bf16[1,64,2048]{2,1,0:T(8,128)(2,1)} %param.10) | copy-start | bytes 786436
  676.8 1.9 copy-start.9
Sparse Core Ops, SparseCore 0:
  13.9 13.0 all-gather.7
  29.1 101.8 all-gather.9
  133.1 243.0 all-gather.11
  378.1 225.9 all-gather.13
  615.9 7.7 reduce-scatter.1
